TPU v7x, 32 devices: a whole 2x2x4 slice. The times are simulated.
32 devices in a mesh: seq: 8 (over z, y), head: 4 (over x, core).
Axes of the slice: x: 2, y: 2, z: 4, core: 2. Of those that a mesh axis runs over, the one named last changes fastest.
Arguments:
- layer_input: bfloat16 [4, 1024, 8192], P('head', 'seq'), may hold values from -6 to 6
- out_grad: bfloat16 [4, 1024, 8192], P('head', 'seq'), may hold values from -6 to 6
- attention_out: bfloat16 [4, 1024, 4096], P('head', 'seq'), may hold values from -6 to 6
- frozen_output_grad: bfloat16 [4, 1024, 4096], P('head', 'seq'), may hold values from -6 to 6
- query_rows: bfloat16 [4, 1024, 4096], P('head', 'seq'), may hold values from -120 to 120
- key_rows: bfloat16 [4, 1024, 512], P('head', 'seq'), may hold values from -4 to 4
- value_rows: bfloat16 [4, 1024, 512], P('head', 'seq'), may hold values from -6 to 6
- seg_lengths: int32 [4, 8], P('head'), may hold values from 1 to 256, 1024 in all within a row
- use_list: int32 [4, 8], replicated, may hold values from 0 to 31, as said below
- store_map: int32 [32], replicated, may hold values from 0 to 31, as said below
- query_down: float32 [32, 64, 8192], P('head', None, 'seq'), may hold values from -0.0625 to 0.0625
- query_up: float32 [32, 64, 4096], P('head', None, 'seq'), may hold values from -0.75 to 0.75
- output_down: float32 [32, 64, 4096], P('head', None, 'seq'), may hold values from -0.09375 to 0.09375
- output_up: float32 [32, 64, 8192], P('head', None, 'seq'), may hold values from -0.75 to 0.75
Outputs:
- grad_query_down: float32 [32, 64, 8192], P('head', None, 'seq')
- grad_query_up: float32 [32, 64, 4096], P('head', None, 'seq')
- grad_output_down: float32 [32, 64, 4096], P('head', None, 'seq')
- grad_output_up: float32 [32, 64, 8192], P('head', None, 'seq')
Inputs may be any that keep to these rules, and one draw needn't show every extreme that they name: `use_list`: each row names 8 distinct tenants. Counting a tenant's store index as store_map[tenant] // 8, a row names at most 2 tenants of one store index, and exactly 2 of some store index in every row. A permutation: tenant t's adapters are in slot store_map[t]. `seg_lengths`: each row sums to 1024.
All inputs are finite; a program needn't handle non-finite values.
Results may differ from a plain program's by a relative error of at most 0.024.
Values may be sent and summed in bfloat16 or wider, within the bound.
A program may use at most 128 MiB of HBM per device.

v0:
```python
import math

import jax
import jax.numpy as jnp
from jax import lax
from jax.sharding import PartitionSpec as P

QH = 32
KVH = 4
HD = 128
CAP = 2


adapter_scale = 2.0
big_negative = -1e30
highest = lax.Precision.HIGHEST


def contract_axes(left_side, right_side, left_dim, right_dim):
    return lax.dot_general(
        left_side,
        right_side,
        (((left_dim,), (right_dim,)), ((), ())),
        preferred_element_type=jnp.float32,
    )


def narrow(full_rows, tenant_row_mask, rank_size):
    length, used_count = tenant_row_mask.shape
    return jnp.sum(
        full_rows.reshape(length, used_count, rank_size) * tenant_row_mask[:, :, None], axis=1
    )


def widened_rows(low_rows, tenant_row_mask):
    length, used_count = tenant_row_mask.shape
    spread_rows = tenant_row_mask.astype(jnp.bfloat16)[:, :, None] * low_rows[:, None, :]
    return spread_rows.reshape(length, used_count * low_rows.shape[1])


def request_tables(use_list, store_map, slots_dev):
    tenants = store_map.shape[0]
    used_count = use_list.shape[1]
    matches = use_list[:, :, None] == jnp.arange(tenants, dtype=jnp.int32)[None, None, :]
    slot_index = jnp.sum(jnp.where(matches, store_map[None, None, :], 0), axis=2)
    owner_index = slot_index // slots_dev
    local_slot = slot_index % slots_dev
    same_owner = (owner_index[:, :, None] == owner_index[:, None, :]).astype(jnp.int32)
    indices = jnp.arange(used_count, dtype=jnp.int32)
    earlier = (indices[None, :] < indices[:, None]).astype(jnp.int32)
    rank_index = jnp.sum(same_owner * earlier[None, :, :], axis=2)
    return (owner_index, local_slot, rank_index)


def attention_grad(query_heads, key_heads, value_heads, gradient_heads, segment, key_span):
    length, head_count, head_width = query_heads.shape
    block_rows = min(512, length)
    window = block_rows + key_span
    factor = 1.0 / math.sqrt(head_width)
    padded_keys = jnp.pad(key_heads, ((key_span, 0), (0, 0), (0, 0)))
    padded_values = jnp.pad(value_heads, ((key_span, 0), (0, 0), (0, 0)))
    padded_segment = jnp.concatenate([jnp.full((key_span,), -1, jnp.int32), segment])

    def one_block(row_start):
        query_block = lax.dynamic_slice_in_dim(query_heads, row_start, block_rows, 0)
        grad_block = lax.dynamic_slice_in_dim(gradient_heads, row_start, block_rows, 0)
        key_block = lax.dynamic_slice_in_dim(padded_keys, row_start, window, 0)
        value_block = lax.dynamic_slice_in_dim(padded_values, row_start, window, 0)
        query_segment = lax.dynamic_slice_in_dim(segment, row_start, block_rows, 0)
        key_segment = lax.dynamic_slice_in_dim(padded_segment, row_start, window, 0)
        query_pos = row_start + jnp.arange(block_rows, dtype=jnp.int32)
        key_pos = row_start - key_span + jnp.arange(window, dtype=jnp.int32)
        allowed = (query_segment[:, None] == key_segment[None, :]) & (
            key_pos[None, :] <= query_pos[:, None]
        )
        scores = (
            jnp.einsum("qhd,khd->hqk", query_block, key_block, preferred_element_type=jnp.float32)
            * factor
        )
        scores = jnp.where(allowed[None, :, :], scores, big_negative)
        row_max = jnp.max(scores, axis=2, keepdims=True)
        weights = jnp.exp(scores - row_max)
        probabilities = weights / jnp.sum(weights, axis=2, keepdims=True)
        prob_grad = jnp.einsum(
            "qhd,khd->hqk", grad_block, value_block, preferred_element_type=jnp.float32
        )
        inner = jnp.sum(probabilities * prob_grad, axis=2, keepdims=True)
        score_grad = (probabilities * (prob_grad - inner)).astype(jnp.bfloat16)
        query_gradient = (
            jnp.einsum("hqk,khd->qhd", score_grad, key_block, preferred_element_type=jnp.float32)
            * factor
        )
        return query_gradient.astype(jnp.bfloat16)

    starts = jnp.arange(0, length, block_rows, dtype=jnp.int32)
    return lax.map(one_block, starts).reshape(length, head_count * head_width)


def shards(
    layer_input,
    out_grad,
    attention_out,
    frozen_output_grad,
    query_rows,
    key_rows,
    value_rows,
    seg_lengths,
    use_list,
    store_map,
    query_down,
    query_up,
    output_down,
    output_up,
):
    slots_dev = query_down.shape[0]
    rank_size = query_down.shape[1]
    group_size = QH // KVH
    input_columns, gradient_columns, head_outputs, base_heads, query_heads = (
        lax.all_to_all(layer_input[0], "seq", split_axis=1, concat_axis=0, tiled=True),
        lax.all_to_all(out_grad[0], "seq", split_axis=1, concat_axis=0, tiled=True),
        lax.all_to_all(attention_out[0], "seq", split_axis=1, concat_axis=0, tiled=True),
        lax.all_to_all(frozen_output_grad[0], "seq", split_axis=1, concat_axis=0, tiled=True),
        lax.all_to_all(query_rows[0], "seq", split_axis=1, concat_axis=0, tiled=True),
    )
    length = input_columns.shape[0]
    heads_here = query_heads.shape[1] // HD
    first_head = lax.axis_index("seq") * heads_here
    gathered_keys, gathered_values = (
        lax.all_gather(key_rows[0], "seq", axis=0, tiled=True),
        lax.all_gather(value_rows[0], "seq", axis=0, tiled=True),
    )
    kv_index = (first_head + jnp.arange(heads_here, dtype=jnp.int32)) // group_size
    key_heads = jnp.take(gathered_keys.reshape(length, KVH, HD), kv_index, axis=1)
    value_heads = jnp.take(gathered_values.reshape(length, KVH, HD), kv_index, axis=1)
    owner_index, local_slot, rank_index = request_tables(use_list, store_map, slots_dev)
    my_index = lax.axis_index("head")
    batch_count = use_list.shape[0]
    cap_ids = jnp.arange(CAP, dtype=jnp.int32)
    slot_ids = jnp.arange(slots_dev, dtype=jnp.int32)
    matched = (
        (owner_index == my_index)[:, :, None, None]
        & (rank_index[:, :, None, None] == cap_ids[None, None, :, None])
        & (local_slot[:, :, None, None] == slot_ids[None, None, None, :])
    )
    select = jnp.sum(matched.astype(jnp.float32), axis=1)

    def pack_slots(store_part):
        return jnp.einsum("mcl,lrw->mcrw", select, store_part, precision=highest).astype(
            jnp.bfloat16
        )

    fetched = (
        lax.all_to_all(pack_slots(query_down), "head", split_axis=0, concat_axis=0, tiled=True),
        lax.all_to_all(pack_slots(query_up), "head", split_axis=0, concat_axis=0, tiled=True),
        lax.all_to_all(pack_slots(output_down), "head", split_axis=0, concat_axis=0, tiled=True),
        lax.all_to_all(pack_slots(output_up), "head", split_axis=0, concat_axis=0, tiled=True),
    )
    mine_owner = lax.dynamic_index_in_dim(owner_index, my_index, 0, keepdims=False)
    mine_rank = lax.dynamic_index_in_dim(rank_index, my_index, 0, keepdims=False)
    store_ids = jnp.arange(batch_count, dtype=jnp.int32)
    picker = (
        (mine_owner[:, None, None] == store_ids[None, :, None])
        & (mine_rank[:, None, None] == cap_ids[None, None, :])
    ).astype(jnp.float32)
    picker_half = picker.astype(jnp.bfloat16)

    def unpack(received):
        chosen = jnp.einsum(
            "ijc,jcrw->irw", picker_half, received, preferred_element_type=jnp.float32
        ).astype(jnp.bfloat16)
        return chosen.reshape(chosen.shape[0] * chosen.shape[1], chosen.shape[2])

    flattened_list = [unpack(received) for received in fetched]
    lengths = seg_lengths[0]
    used_count = lengths.shape[0]
    offsets = jnp.cumsum(lengths) - lengths
    positions = jnp.arange(length, dtype=jnp.int32)
    segment = jnp.sum((positions[:, None] >= offsets[None, :]).astype(jnp.int32), axis=1) - 1
    tenant_row_mask = (segment[:, None] == jnp.arange(used_count, dtype=jnp.int32)[None, :]).astype(
        jnp.float32
    )
    partial_out = narrow(
        contract_axes(head_outputs, flattened_list[2], 1, 1), tenant_row_mask, rank_size
    )
    partial_grad = narrow(
        contract_axes(gradient_columns, flattened_list[3], 1, 1), tenant_row_mask, rank_size
    )
    partial_query = narrow(
        contract_axes(input_columns, flattened_list[0], 1, 1), tenant_row_mask, rank_size
    )
    summed_out, summed_grad, summed_query = (
        lax.psum(partial_out.astype(jnp.bfloat16), "seq").astype(jnp.float32),
        lax.psum(partial_grad.astype(jnp.bfloat16), "seq").astype(jnp.float32),
        lax.psum(partial_query.astype(jnp.bfloat16), "seq").astype(jnp.float32),
    )
    low_rank_output = summed_out.astype(jnp.bfloat16)
    low_grad = summed_grad.astype(jnp.bfloat16)
    low_rank_query = summed_query.astype(jnp.bfloat16)
    widened_gradient = widened_rows(low_grad, tenant_row_mask)
    gradient_heads = (
        base_heads.astype(jnp.float32)
        + adapter_scale
        * jnp.dot(widened_gradient, flattened_list[2], preferred_element_type=jnp.float32)
    ).astype(jnp.bfloat16)
    query_gradient = attention_grad(
        query_heads.reshape(length, heads_here, HD),
        key_heads,
        value_heads,
        gradient_heads.reshape(length, heads_here, HD),
        segment,
        length // 4,
    )
    partial_back = narrow(
        contract_axes(query_gradient, flattened_list[1], 1, 1), tenant_row_mask, rank_size
    )
    low_rank_back = lax.psum(partial_back.astype(jnp.bfloat16), "seq")
    outer_products = (
        adapter_scale
        * contract_axes(widened_rows(low_rank_back, tenant_row_mask), input_columns, 0, 0),
        adapter_scale
        * contract_axes(widened_rows(low_rank_query, tenant_row_mask), query_gradient, 0, 0),
        adapter_scale * contract_axes(widened_gradient, head_outputs, 0, 0),
        adapter_scale
        * contract_axes(widened_rows(low_rank_output, tenant_row_mask), gradient_columns, 0, 0),
    )

    def spread(gradient):
        pieces = gradient.reshape(used_count, rank_size, gradient.shape[1])
        return jnp.einsum("ijc,irw->jcrw", picker, pieces, precision=highest)

    returned = (
        lax.all_to_all(
            spread(outer_products[0]).astype(jnp.bfloat16),
            "head",
            split_axis=0,
            concat_axis=0,
            tiled=True,
        ).astype(jnp.float32),
        lax.all_to_all(
            spread(outer_products[1]).astype(jnp.bfloat16),
            "head",
            split_axis=0,
            concat_axis=0,
            tiled=True,
        ).astype(jnp.float32),
        lax.all_to_all(
            spread(outer_products[2]).astype(jnp.bfloat16),
            "head",
            split_axis=0,
            concat_axis=0,
            tiled=True,
        ).astype(jnp.float32),
        lax.all_to_all(
            spread(outer_products[3]).astype(jnp.bfloat16),
            "head",
            split_axis=0,
            concat_axis=0,
            tiled=True,
        ).astype(jnp.float32),
    )

    def settle(received):
        return jnp.einsum("mcl,mcrw->lrw", select, received, precision=highest)

    return (settle(returned[0]), settle(returned[1]), settle(returned[2]), settle(returned[3]))


def solution(mesh):
    placed = (
        P("head", "seq", None),
        P("head", "seq", None),
        P("head", "seq", None),
        P("head", "seq", None),
        P("head", "seq", None),
        P("head", "seq", None),
        P("head", "seq", None),
        P("head", None),
        P(),
        P(),
        P("head", None, "seq"),
        P("head", None, "seq"),
        P("head", None, "seq"),
        P("head", None, "seq"),
    )
    return jax.shard_map(
        shards,
        mesh=mesh,
        in_specs=placed,
        out_specs=(
            P("head", None, "seq"),
            P("head", None, "seq"),
            P("head", None, "seq"),
            P("head", None, "seq"),
        ),
        check_vma=False,
    )
```

profile of v0, /device:TPU:1, one launch (start us, length us, event | category | flops | bytes accessed | tf_op | source)
XLA Modules:
  0.0 578.2 jit_solution(9823844953946376288)
XLA Ops:
  8.7 3.1 convolution_convert_fusion.1
  13.1 4.3 all-to-all-start.4
  20.1 5.4 all-to-all-done.4
  25.5 4.7 all-to-all-start.5
  30.2 3.8 fusion.31
  39.0 4.6 all-to-all-start.2
  43.6 5.4 fusion.34
  50.8 6.4 %all-to-all-done.2 = bf16[4,2,64,1024]{3,1,2,0:T(2,128)(2,1)S(1)} async-done(((bf16[4,2,64,1024]{3,1,2,0:T(2,128)(2,1)}), bf16[4,2,64,1024]{3,1,2,0:T(2,128)(2,1)S(1)}, u32[]{:S(2)}, u32[]{:S(2)}) %all-to-all-start.2) | async-done | bytes 1048608 | tf_op jit(solution)/shard_map/all_to_all | solution.py:156
  58.1 4.4 all-to-all-start.8
  63.8 12.3 %all-to-all-done.8 = bf16[4,2,64,1024]{3,1,2,0:T(2,128)(2,1)S(1)} async-done(((bf16[4,2,64,1024]{3,1,2,0:T(2,128)(2,1)}), bf16[4,2,64,1024]{3,1,2,0:T(2,128)(2,1)S(1)}, u32[]{:S(2)}, u32[]{:S(2)}) %all-to-all-start.8) | async-done | bytes 1048608 | tf_op jit(solution)/shard_map/all_to_all | solution.py:153
  77.0 6.4 %all-to-all-start.10 = ((bf16[128,8,512]{0,2,1:T(8,128)(2,1)}), bf16[128,8,512]{0,2,1:T(8,128)(2,1)S(1)}, u32[]{:S(2)}, u32[]{:S(2)}) async-start(bf16[128,8,512]{0,2,1:T(8,128)(2,1)} %bitcast.60), calls=%async_computation.10 | async-start | bytes 2097152 | tf_op jit(solution)/shard_map/all_to_all | solution.py:121
  84.7 23.3 %all-to-all-done.10 = bf16[128,8,512]{0,2,1:T(8,128)(2,1)S(1)} async-done(((bf16[128,8,512]{0,2,1:T(8,128)(2,1)}), bf16[128,8,512]{0,2,1:T(8,128)(2,1)S(1)}, u32[]{:S(2)}, u32[]{:S(2)}) %all-to-all-start.10) | async-done | bytes 1048608 | tf_op jit(solution)/shard_map/all_to_all | solution.py:121
  108.0 5.0 all-to-all-start
  113.0 4.1 copy.137
  117.0 21.0 %all-to-all-done = bf16[128,8,512]{0,2,1:T(8,128)(2,1)S(1)} async-done(((bf16[128,8,512]{0,2,1:T(8,128)(2,1)}), bf16[128,8,512]{0,2,1:T(8,128)(2,1)S(1)}, u32[]{:S(2)}, u32[]{:S(2)}) %all-to-all-start) | async-done | bytes 1048608 | tf_op jit(solution)/shard_map/all_to_all | solution.py:123
  139.0 4.5 all-to-all-start.3
  144.3 4.1 copy.154
  148.4 50.5 %all-to-all-done.3 = bf16[128,8,1024]{0,2,1:T(8,128)(2,1)S(1)} async-done(((bf16[128,8,1024]{0,2,1:T(8,128)(2,1)}), bf16[128,8,1024]{0,2,1:T(8,128)(2,1)S(1)}, u32[]{:S(2)}, u32[]{:S(2)}) %all-to-all-start.3) | async-done | bytes 2097184 | tf_op jit(solution)/shard_map/all_to_all | solution.py:120
  200.2 6.6 %all-to-all-start.6 = ((bf16[128,8,1024]{0,2,1:T(8,128)(2,1)}), bf16[128,8,1024]{0,2,1:T(8,128)(2,1)}, u32[]{:S(2)}, u32[]{:S(2)}) async-start(bf16[128,8,1024]{0,2,1:T(8,128)(2,1)} %bitcast.183), calls=%async_computation.6 | async-start | bytes 4194304 | tf_op jit(solution)/shard_map/all_to_all | solution.py:119
  216.9 45.4 %all-to-all-done.6 = bf16[128,8,1024]{0,2,1:T(8,128)(2,1)} async-done(((bf16[128,8,1024]{0,2,1:T(8,128)(2,1)}), bf16[128,8,1024]{0,2,1:T(8,128)(2,1)}, u32[]{:S(2)}, u32[]{:S(2)}) %all-to-all-start.6) | async-done | bytes 2097184 | tf_op jit(solution)/shard_map/all_to_all | solution.py:119
  262.4 6.7 %all-to-all-start.1 = ((bf16[128,8,512]{0,2,1:T(8,128)(2,1)}), bf16[128,8,512]{0,2,1:T(8,128)(2,1)}, u32[]{:S(2)}, u32[]{:S(2)}) async-start(bf16[128,8,512]{0,2,1:T(8,128)(2,1)} %bitcast.12), calls=%async_computation.1 | async-start | bytes 2097152 | tf_op jit(solution)/shard_map/all_to_all | solution.py:122
  283.0 3.9 copy.138
  286.9 3.9 copy.155
  290.8 3.3 fusion.80
  302.2 63.5 %all-reduce.7.cloned.1.call-done = bf16[1024,64]{0,1:T(8,128)(2,1)} async-done(((bf16[1024,64]{0,1:T(8,128)(2,1)}), bf16[1024,64]{0,1:T(8,128)(2,1)}) %all-reduce.7.cloned.1.call-update) | async-done | bytes 131088 | tf_op jit(solution)/shard_map/psum | solution.py:193
  365.7 3.0 fusion.22
  368.8 50.4 %while.12 = (s32[]{:T(128)}, bf16[2,512,4,128]{3,2,1,0:T(4,128)(2,1)}, s32[2]{0:T(128)S(1)}, bf16[1280,4,128]{2,0,1:T(8,128)(2,1)S(1)}, s32[1024]{0:T(1024)S(1)}...) while((s32[]{:T(128)}, ...), condition=%wide.region_11.13_spmd, body=%wide.region_7.12_spmd.sunk | while | flops 1230110720 | bytes 50923260 | solution.py:96
  372.8 5.1 fusion.110
  379.8 7.7 %fusion.111 = (f32[4,512]{1,0:T(4,128)S(1)}, f32[4,512,768]{2,1,0:T(8,128)S(1)}) fusion(f32[4,512,768]{2,1,0:T(8,128)} %fusion.110, pred[512,768]{1,0:T(8,128)(4,1)S(1)} %compare_and_fusion.4), kind=kOutput, calls=%fused_computation.141.clone.1 | output fusion | flops 9437951 | bytes 12984320 | tf_op jit(solution)/shard_map/while/body/eval_jaxpr/sub | solution.py:82
  387.5 3.4 multiply_reduce_fusion.6
  398.0 5.0 fusion.110
  405.0 7.7 %fusion.111 = (f32[4,512]{1,0:T(4,128)S(1)}, f32[4,512,768]{2,1,0:T(8,128)S(1)}) fusion(f32[4,512,768]{2,1,0:T(8,128)} %fusion.110, pred[512,768]{1,0:T(8,128)(4,1)S(1)} %compare_and_fusion.4), kind=kOutput, calls=%fused_computation.141.clone.1 | output fusion | flops 9437951 | bytes 12984320 | tf_op jit(solution)/shard_map/while/body/eval_jaxpr/sub | solution.py:82
  412.7 3.4 multiply_reduce_fusion.6
  422.1 71.7 %all-reduce.9.cloned.1.call-done = (bf16[1024,64]{0,1:T(8,128)(2,1)}, bf16[1024,64]{0,1:T(8,128)(2,1)}, bf16[1024,64]{0,1:T(8,128)(2,1)}) async-done(((bf16[1024,64]{0,1:T(8,128)(2,1)}, bf16[1024,64]{0,1:T(8,128)(2,1)}, bf16[1024,64]{0,1:T(8,128)(2,1)}), (bf16[1024,64]{0,1:T(8,128)(2,1)}, bf16[1024,64]{0,1:T(8,128)(2,1)}, bf16[1024,64]{0,1:T(8,128)(2,1)})) %all-reduce.9.cloned.1.call-update) | async-done | bytes 393232 | tf_op jit(solution)/shard_map/psum | solution.py:216
  493.8 2.8 broadcast_multiply_fusion
  499.9 6.4 %all-to-all-start.9 = ((bf16[4,2,64,512]{3,1,2,0:T(2,128)(2,1)}), bf16[4,2,64,512]{3,1,2,0:T(2,128)(2,1)}, u32[]{:S(2)}, u32[]{:S(2)}) async-start(bf16[4,2,64,512]{3,1,2,0:T(2,128)(2,1)} %copy.166), calls=%async_computation.9 | async-start | bytes 1048576 | tf_op jit(solution)/shard_map/all_to_all | solution.py:239
  510.9 3.5 all-to-all-done.9
  514.4 5.0 all-to-all-start.11
  520.6 2.8 fusion.40
  527.4 4.4 all-to-all-start.12
  531.8 2.5 convolution_multiply_fusion.1
  534.3 2.8 fusion.37
  538.8 6.5 %all-to-all-done.12 = bf16[4,2,64,1024]{3,1,2,0:T(2,128)(2,1)S(1)} async-done(((bf16[4,2,64,1024]{3,1,2,0:T(2,128)(2,1)}), bf16[4,2,64,1024]{3,1,2,0:T(2,128)(2,1)S(1)}, u32[]{:S(2)}, u32[]{:S(2)}) %all-to-all-start.12) | async-done | bytes 1048608 | tf_op jit(solution)/shard_map/all_to_all | solution.py:253
  545.4 5.3 all-to-all-start.7
  558.8 2.7 convolution_bitcast_fusion
  561.5 2.5 copy.183
  564.4 4.3 convolution_bitcast_fusion.1
  568.7 2.5 copy.180
  (159 shorter events, 88.0 us)
Async XLA Ops:
  7.2 23.1 %copy-start = (f32[8,64,1024]{2,1,0:T(8,128)S(1)}, f32[8,64,1024]{2,1,0:T(8,128)}, u32[]{:S(2)}) copy-start(f32[8,64,1024]{2,1,0:T(8,128)} %param.31) | copy-start | bytes 6291460
  7.2 10.1 %copy-start.9 = (f32[8,64,512]{2,1,0:T(8,128)S(1)}, f32[8,64,512]{2,1,0:T(8,128)}, u32[]{:S(2)}) copy-start(f32[8,64,512]{2,1,0:T(8,128)} %param.29) | copy-start | bytes 3145732
  8.7 34.8 %copy-start.26 = (f32[4,2,8]{2,1,0:T(2,128)}, f32[4,2,8]{2,1,0:T(2,128)S(1)}, u32[]{:S(2)}) copy-start(f32[4,2,8]{2,1,0:T(2,128)S(1)} %convert_reduce_fusion.1) | copy-start | bytes 772
  13.1 12.5 %all-to-all-start.4 = ((bf16[4,2,64,512]{3,1,2,0:T(2,128)(2,1)}), bf16[4,2,64,512]{3,1,2,0:T(2,128)(2,1)}, u32[]{:S(2)}, u32[]{:S(2)}) async-start(bf16[4,2,64,512]{3,1,2,0:T(2,128)(2,1)} %copy.141), calls=%async_computation.4 | async-start | bytes 1048576 | tf_op jit(solution)/shard_map/all_to_all | solution.py:155
  25.5 12.6 %all-to-all-start.5 = ((bf16[4,2,64,512]{3,2,1,0:T(8,128)(2,1)}), bf16[4,2,64,512]{3,2,1,0:T(8,128)(2,1)S(1)}, u32[]{:S(2)}, u32[]{:S(2)}) async-start(bf16[4,2,64,512]{3,2,1,0:T(8,128)(2,1)} %copy.151), calls=%async_computation.5 | async-start | bytes 1048576 | tf_op jit(solution)/shard_map/all_to_all | solution.py:154
  38.2 0.8 copy-start.19
  39.0 18.1 %all-to-all-start.2 = ((bf16[4,2,64,1024]{3,1,2,0:T(2,128)(2,1)}), bf16[4,2,64,1024]{3,1,2,0:T(2,128)(2,1)S(1)}, u32[]{:S(2)}, u32[]{:S(2)}) async-start(bf16[4,2,64,1024]{3,1,2,0:T(2,128)(2,1)} %copy.134), calls=%async_computation.2 | async-start | bytes 2097152 | tf_op jit(solution)/shard_map/all_to_all | solution.py:156
  49.0 13.5 %copy-start.10 = (bf16[1,128,4096]{2,1,0:T(8,128)(2,1)S(1)}, bf16[1,128,4096]{2,1,0:T(8,128)(2,1)}, u32[]{:S(2)}) copy-start(bf16[1,128,4096]{2,1,0:T(8,128)(2,1)} %param.20) | copy-start | bytes 3145732
  57.1 1.0 copy-start.15
  58.1 18.0 %all-to-all-start.8 = ((bf16[4,2,64,1024]{3,1,2,0:T(2,128)(2,1)}), bf16[4,2,64,1024]{3,1,2,0:T(2,128)(2,1)S(1)}, u32[]{:S(2)}, u32[]{:S(2)}) async-start(bf16[4,2,64,1024]{3,1,2,0:T(2,128)(2,1)} %copy.162), calls=%async_computation.8 | async-start | bytes 2097152 | tf_op jit(solution)/shard_map/all_to_all | solution.py:153
  62.5 20.9 %copy-start.11 = (bf16[1,128,4096]{2,1,0:T(8,128)(2,1)S(1)}, bf16[1,128,4096]{2,1,0:T(8,128)(2,1)}, u32[]{:S(2)}) copy-start(bf16[1,128,4096]{2,1,0:T(8,128)(2,1)} %param.22) | copy-start | bytes 3145732
  76.1 1.0 copy-start.13
  77.0 31.0 %all-to-all-start.10 = ((bf16[128,8,512]{0,2,1:T(8,128)(2,1)}), bf16[128,8,512]{0,2,1:T(8,128)(2,1)S(1)}, u32[]{:S(2)}, u32[]{:S(2)}) async-start(bf16[128,8,512]{0,2,1:T(8,128)(2,1)} %bitcast.60), calls=%async_computation.10 | async-start | bytes 2097152 | tf_op jit(solution)/shard_map/all_to_all | solution.py:121
  108.0 30.1 %all-to-all-start = ((bf16[128,8,512]{0,2,1:T(8,128)(2,1)}), bf16[128,8,512]{0,2,1:T(8,128)(2,1)S(1)}, u32[]{:S(2)}, u32[]{:S(2)}) async-start(bf16[128,8,512]{0,2,1:T(8,128)(2,1)} %bitcast.10), calls=%async_computation | async-start | bytes 2097152 | tf_op jit(solution)/shard_map/all_to_all | solution.py:123
  138.1 1.0 copy-start.4
  138.1 5.5 copy-start.24
  139.0 59.9 %all-to-all-start.3 = ((bf16[128,8,1024]{0,2,1:T(8,128)(2,1)}), bf16[128,8,1024]{0,2,1:T(8,128)(2,1)S(1)}, u32[]{:S(2)}, u32[]{:S(2)}) async-start(bf16[128,8,1024]{0,2,1:T(8,128)(2,1)} %bitcast.184), calls=%async_computation.3 | async-start | bytes 4194304 | tf_op jit(solution)/shard_map/all_to_all | solution.py:120
  143.5 131.7 %all-gather.5.cloned.1.call-start = ((), (), s32[]{:S(2)}) async-start(), calls=%async_computation.14 | async-start | bytes 1179648 | tf_op jit(solution)/shard_map/all_gather | solution.py:129
  198.9 1.3 copy-start.2
  198.9 8.0 %copy-start.25 = (bf16[1,128,512]{2,1,0:T(8,128)(2,1)S(1)}, bf16[1,128,512]{2,1,0:T(8,128)(2,1)}, u32[]{:S(2)}) copy-start(bf16[1,128,512]{2,1,0:T(8,128)(2,1)} %param.24) | copy-start | bytes 393220
  198.9 8.8 %copy-start.28 = (s32[1,8]{1,0:T(1,128)S(1)}, s32[1,8]{1,0:T(1,128)}, u32[]{:S(2)}) copy-start(s32[1,8]{1,0:T(1,128)} %param.25) | copy-start | bytes 100
  200.2 62.1 %all-to-all-start.6 = ((bf16[128,8,1024]{0,2,1:T(8,128)(2,1)}), bf16[128,8,1024]{0,2,1:T(8,128)(2,1)}, u32[]{:S(2)}, u32[]{:S(2)}) async-start(bf16[128,8,1024]{0,2,1:T(8,128)(2,1)} %bitcast.183), calls=%async_computation.6 | async-start | bytes 4194304 | tf_op jit(solution)/shard_map/all_to_all | solution.py:119
  206.8 70.0 %all-gather.7.cloned.1.call-start = ((), (), s32[]{:S(2)}) async-start(), calls=%async_computation.15 | async-start | bytes 1179648 | tf_op jit(solution)/shard_map/all_gather | solution.py:130
  207.9 5.4 copy-start.20
  210.2 4.5 copy-start.16
  212.2 1.0 copy-start.21
  214.7 54.8 %copy-start.14 = (bf16[4,2,64,1024]{3,1,2,0:T(2,128)(2,1)S(1)}, bf16[4,2,64,1024]{3,1,2,0:T(2,128)(2,1)}, u32[]{:S(2)}) copy-start(bf16[4,2,64,1024]{3,1,2,0:T(2,128)(2,1)} %copy-done.13) | copy-start | bytes 3145732
  262.4 8.4 %copy-start.18 = (bf16[8,64,1024]{2,0,1:T(8,128)(2,1)S(1)}, bf16[8,64,1024]{2,0,1:T(8,128)(2,1)}, u32[]{:S(2)}) copy-start(bf16[8,64,1024]{2,0,1:T(8,128)(2,1)} %bitcast_convert_fusion.1) | copy-start | bytes 3145732
  262.4 39.8 %all-to-all-start.1 = ((bf16[128,8,512]{0,2,1:T(8,128)(2,1)}), bf16[128,8,512]{0,2,1:T(8,128)(2,1)}, u32[]{:S(2)}, u32[]{:S(2)}) async-start(bf16[128,8,512]{0,2,1:T(8,128)(2,1)} %bitcast.12), calls=%async_computation.1 | async-start | bytes 2097152 | tf_op jit(solution)/shard_map/all_to_all | solution.py:122
  269.0 96.7 %all-reduce.7.cloned.1.call-start = ((), (), s32[]{:S(2)}) async-start(), calls=%async_computation.13 | async-start | bytes 262144 | tf_op jit(solution)/shard_map/psum | solution.py:193
  290.8 3.4 copy-start.6
  290.8 3.4 copy-start.17
  297.1 196.7 %all-reduce.9.cloned.1.call-start = ((), (), s32[]{:S(2)}) async-start(), calls=%async_computation.16 | async-start | bytes 786432 | tf_op jit(solution)/shard_map/psum | solution.py:216
  298.6 1.4 copy-start.5
  300.1 65.7 %copy-start.22 = (bf16[8,64,512]{2,0,1:T(8,128)(2,1)S(1)}, bf16[8,64,512]{2,0,1:T(8,128)(2,1)}, u32[]{:S(2)}) copy-start(bf16[8,64,512]{2,0,1:T(8,128)(2,1)} %copy-done.21) | copy-start | bytes 1572868
  419.1 1.5 copy-start.29
  420.7 73.1 %copy-start.23 = (bf16[1024,64]{0,1:T(8,128)(2,1)S(1)}, bf16[1024,64]{0,1:T(8,128)(2,1)}, u32[]{:S(2)}) copy-start(bf16[1024,64]{0,1:T(8,128)(2,1)} %all-reduce.7.cloned.1.call-done) | copy-start | bytes 393220
  493.8 2.8 copy-start.12
  497.3 9.1 %copy-start.3 = (bf16[8,128,512]{2,1,0:T(8,128)(2,1)S(1)}, bf16[8,128,512]{2,1,0:T(8,128)(2,1)}, u32[]{:S(2)}) copy-start(bf16[8,128,512]{2,1,0:T(8,128)(2,1)} %copy.170) | copy-start | bytes 3145732
  499.9 14.5 %all-to-all-start.9 = ((bf16[4,2,64,512]{3,1,2,0:T(2,128)(2,1)}), bf16[4,2,64,512]{3,1,2,0:T(2,128)(2,1)}, u32[]{:S(2)}, u32[]{:S(2)}) async-start(bf16[4,2,64,512]{3,1,2,0:T(2,128)(2,1)} %copy.166), calls=%async_computation.9 | async-start | bytes 1048576 | tf_op jit(solution)/shard_map/all_to_all | solution.py:239
  508.3 11.1 %copy-start.8 = (bf16[8,128,1024]{2,1,0:T(8,128)(2,1)S(1)}, bf16[8,128,1024]{2,1,0:T(8,128)(2,1)}, u32[]{:S(2)}) copy-start(bf16[8,128,1024]{2,1,0:T(8,128)(2,1)} %copy.138) | copy-start | bytes 6291460
  514.4 13.1 %all-to-all-start.11 = ((bf16[4,2,64,512]{3,1,2,0:T(2,128)(2,1)}), bf16[4,2,64,512]{3,1,2,0:T(2,128)(2,1)}, u32[]{:S(2)}, u32[]{:S(2)}) async-start(bf16[4,2,64,512]{3,1,2,0:T(2,128)(2,1)} %copy.172), calls=%async_computation.11 | async-start | bytes 1048576 | tf_op jit(solution)/shard_map/all_to_all | solution.py:246
  525.2 6.6 %copy-start.7 = (bf16[8,128,1024]{2,1,0:T(8,128)(2,1)S(1)}, bf16[8,128,1024]{2,1,0:T(8,128)(2,1)}, u32[]{:S(2)}) copy-start(bf16[8,128,1024]{2,1,0:T(8,128)(2,1)} %copy.155) | copy-start | bytes 6291460
  527.4 18.0 %all-to-all-start.12 = ((bf16[4,2,64,1024]{3,1,2,0:T(2,128)(2,1)}), bf16[4,2,64,1024]{3,1,2,0:T(2,128)(2,1)S(1)}, u32[]{:S(2)}, u32[]{:S(2)}) async-start(bf16[4,2,64,1024]{3,1,2,0:T(2,128)(2,1)} %copy.177), calls=%async_computation.12 | async-start | bytes 2097152 | tf_op jit(solution)/shard_map/all_to_all | solution.py:253
  537.1 13.7 %copy-start.27 = (f32[4,2,8]{2,1,0:T(2,128)S(1)}, f32[4,2,8]{2,1,0:T(2,128)}, u32[]{:S(2)}) copy-start(f32[4,2,8]{2,1,0:T(2,128)} %copy-done.26) | copy-start | bytes 772
  545.4 19.0 %all-to-all-start.7 = ((bf16[4,2,64,1024]{3,1,2,0:T(2,128)(2,1)}), bf16[4,2,64,1024]{3,1,2,0:T(2,128)(2,1)}, u32[]{:S(2)}, u32[]{:S(2)}) async-start(bf16[4,2,64,1024]{3,1,2,0:T(2,128)(2,1)} %copy.157), calls=%async_computation.7 | async-start | bytes 2097152 | tf_op jit(solution)/shard_map/all_to_all | solution.py:232
  564.4 6.8 %copy-start.1 = (f32[8,64,1024]{2,1,0:T(8,128)S(1)}, f32[8,64,1024]{2,1,0:T(8,128)}, u32[]{:S(2)}) copy-start(f32[8,64,1024]{2,1,0:T(8,128)} %param.31) | copy-start | bytes 6291460
Sparse Core Ops, SparseCore 0:
  146.4 58.2 all-gather.4
  209.7 58.1 all-gather.6
  297.2 68.4 all-reduce.6
  422.2 71.4 all-reduce.8
where the time goes:
time: 588 us; the launch traced here: 578 us
  waiting for transfers between devices  315 us (54%)
  matrix products  79.1 us (13%)
  starting transfers between devices  68.6 us (12%)
  local copies, waits for them, and re-layouts  67.7 us (12%)
  other arithmetic  25.2 us (4%)
  between operations  14.7 us (2%)
  loops' own time  8.21 us (1%)
    psum x1, waiting for transfers between devices, shards(): low_rank_back = lax.psum(partial_back.astype(jnp.bfloat16), 'seq')  71.7 us
    psum x1, waiting for transfers between devices, shards(): lax.psum(partial_grad.astype(jnp.bfloat16), 'seq').astype(jnp.float32)  63.5 us
    all_to_all x1, waiting for transfers between devices, shards(): lax.all_to_all(out_grad[0], 'seq', split_axis=1, concat_axis=0, tiled=True)  50.5 us
    all_to_all x1, waiting for transfers between devices, shards(): lax.all_to_all(layer_input[0], 'seq', split_axis=1, concat_axis=0, tiled=...  45.4 us
    unnamed x71, local copies, waits for them, and re-layouts  28.1 us
    all_to_all x1, waiting for transfers between devices, shards(): lax.all_to_all(attention_out[0], 'seq', split_axis=1, concat_axis=0, tile...  23.3 us
    all_to_all x1, waiting for transfers between devices, shards(): lax.all_to_all(query_rows[0], 'seq', split_axis=1, concat_axis=0, tiled=T...  21 us
    sub x2, other arithmetic, one_block(): weights = jnp.exp(scores - row_max)  15.4 us
  transfers between devices with their start and end apart: 17, of which 14 were waited for; matrix products, arithmetic and copies ran while one was open for 17% of the time, Pallas kernels for 0%

commit v1 on v0

v1 whole, which is shorter than its diff:
```python
import functools
import math

import jax
import jax.numpy as jnp
from jax import lax
from jax.experimental import pallas as pl
from jax.experimental.pallas import tpu as pltpu
from jax.sharding import PartitionSpec as P

QH = 32
KVH = 4
HD = 128
CAP = 2
LANES = 128
TILE = 256

adapter_scale = 2.0
big_negative = -1e30
MESH = pl.DeviceIdType.MESH
bf16 = jnp.bfloat16
f32 = jnp.float32


def dot(left_side, right_side, left_dim=1, right_dim=0):
    return lax.dot_general(
        left_side,
        right_side,
        (((left_dim,), (right_dim,)), ((), ())),
        preferred_element_type=f32,
    )


def gradient_kernel(
    n, groups,
    x_ref, g_ref, a_ref, f_ref, q_ref, k_ref, v_ref,
    seg_ref, use_ref, map_ref,
    qd_ref, qu_ref, od_ref, ou_ref,
    rqd_ref, rqu_ref, rod_ref, rou_ref,
    xc, gc, ac, fc, qc, kc, vc,
    sqd, squ, sod, sou,
    kqd, kqu, kod, kou,
    pqd, pqu, pod, pou,
    dqd, dqu, dod, dou,
    part, gathered, low, wide, qg,
    store_sem, tok_send, tok_recv, tok_local,
    pan_send, pan_recv, pan_local,
    rs_send, rs_recv, ag_send, ag_recv,
    ret_send, ret_recv, ret_local,
):
    me = lax.axis_index("seq")
    mine = lax.axis_index("head")
    rows = x_ref.shape[1]
    half = rows // 2
    length = n * rows
    span = length // 4
    window = TILE + span
    slots_dev, rank_size = qd_ref.shape[0], qd_ref.shape[1]
    seat_rows = groups * CAP * rank_size
    used = use_ref.shape[1]
    heads_here = QH // n
    group_size = QH // KVH
    factor = 1.0 / math.sqrt(HD)
    pairs = seat_rows // LANES
    block = CAP * rank_size

    stores = ((qd_ref, sqd), (qu_ref, squ), (od_ref, sod), (ou_ref, sou))
    for i, (source, target) in enumerate(stores):
        pltpu.make_async_copy(source, target, store_sem.at[i]).start()

    barrier = pltpu.get_barrier_semaphore()

    def greet_seq(k, carry):
        pl.semaphore_signal(
            barrier, inc=1, device_id={"seq": lax.rem(me + k, n)}, device_id_type=MESH
        )
        return carry

    def greet_head(k, carry):
        pl.semaphore_signal(
            barrier, inc=1, device_id={"head": lax.rem(mine + k, groups)}, device_id_type=MESH
        )
        return carry

    lax.fori_loop(1, n, greet_seq, 0)
    lax.fori_loop(1, groups, greet_head, 0)
    pl.semaphore_wait(barrier, n + groups - 2)

    def kv_head(p):
        return (p * heads_here) // group_size

    tokens = (
        (g_ref, gc, 0, None),
        (f_ref, fc, 0, None),
        (q_ref, qc, 0, None),
        (k_ref, kc, span, kv_head),
        (v_ref, vc, span, kv_head),
        (a_ref, ac, 0, None),
        (x_ref, xc, 0, None),
    )

    def send_tokens(i):
        source, target, first, head_of = tokens[i]
        width = target.shape[1]

        def view(p):
            column = p if head_of is None else head_of(p)
            return source.at[0, :, pl.ds(pl.multiple_of(column * width, LANES), width)]

        landing = target.at[pl.ds(pl.multiple_of(first + me * rows, rows), rows)]

        def one(k, carry):
            p = lax.rem(me + k, n)
            pltpu.make_async_remote_copy(
                src_ref=view(p), dst_ref=landing, send_sem=tok_send.at[i], recv_sem=tok_recv.at[i],
                device_id={"seq": p}, device_id_type=MESH,
            ).start()
            return carry

        lax.fori_loop(1, n, one, 0)
        pltpu.make_async_copy(view(me), landing, tok_local.at[i]).start()

    def all_bytes(ref, sem):
        pltpu.make_async_copy(ref, ref, sem).wait()

    def token_bytes(i):
        return tokens[i][1].at[pl.ds(0, (n - 1) * rows)]

    def wait_tokens(i):
        all_bytes(token_bytes(i), tok_recv.at[i])
        all_bytes(tokens[i][1].at[pl.ds(0, rows)], tok_local.at[i])

    for i in range(5):
        send_tokens(i)
    kc[pl.ds(0, span), :] = jnp.zeros((span, HD), bf16)
    vc[pl.ds(0, span), :] = jnp.zeros((span, HD), bf16)

    def slot_of(m, i):
        return map_ref[use_ref[m, i]]

    picks = []
    for m in range(groups):
        count = jnp.int32(0)
        index = [jnp.int32(0)] * CAP
        for i in range(used):
            slot = slot_of(m, i)
            hit = (slot // slots_dev) == mine
            for c in range(CAP):
                index[c] = jnp.where(hit & (count == c), slot % slots_dev, index[c])
            count = count + jnp.where(hit, 1, 0)
        picks.append((index, count))

    panels = ((sqd, kqd, pqd), (squ, kqu, pqu), (sod, kod, pod), (sou, kou, pou))

    def send_panels(i):
        store, packed, target = panels[i]
        pltpu.make_async_copy(stores[i][0], store, store_sem.at[i]).wait()
        for m in range(groups):
            index, count = picks[m]
            for c in range(CAP):
                panel = store[index[c]]
                keep = jnp.where(count > c, 1.0, 0.0).astype(f32)
                packed[pl.ds(m * block + c * rank_size, rank_size), :] = (panel * keep).astype(bf16)
        landing = target.at[pl.ds(pl.multiple_of(mine * block, block), block)]

        def one(k, carry):
            p = lax.rem(mine + k, groups)
            pltpu.make_async_remote_copy(
                src_ref=packed.at[pl.ds(pl.multiple_of(p * block, block), block)],
                dst_ref=landing, send_sem=pan_send.at[i], recv_sem=pan_recv.at[i],
                device_id={"head": p}, device_id_type=MESH,
            ).start()
            return carry

        lax.fori_loop(1, groups, one, 0)
        pltpu.make_async_copy(
            packed.at[pl.ds(pl.multiple_of(mine * block, block), block)], landing, pan_local.at[i]
        ).start()

    def wait_panels(i):
        target = panels[i][2]
        all_bytes(target.at[pl.ds(0, (groups - 1) * block)], pan_recv.at[i])
        all_bytes(target.at[pl.ds(0, block)], pan_local.at[i])

    for i in (3, 2, 1, 0):
        send_panels(i)

    owners = [slot_of(mine, i) // slots_dev for i in range(used)]
    seats, offsets, total = [], [], jnp.int32(0)
    for i in range(used):
        rank = jnp.int32(0)
        for j in range(i):
            rank = rank + jnp.where(owners[j] == owners[i], 1, 0)
        seats.append(owners[i] * CAP + rank)
        offsets.append(total)
        total = total + seg_ref[0, i]

    def chosen(positions, values):
        result = jnp.full(positions.shape, values[0], jnp.int32)
        for i in range(1, used):
            result = jnp.where(positions >= offsets[i], values[i], result)
        return result

    def column_positions(tile):
        return tile * TILE + lax.broadcasted_iota(jnp.int32, (TILE, 1), 0)

    upper = (lax.broadcasted_iota(jnp.int32, (1, LANES), 1) >= rank_size).astype(jnp.int32)
    upper_row = (lax.broadcasted_iota(jnp.int32, (LANES, 1), 0) >= rank_size).astype(jnp.int32)

    def at(start, size):
        return pl.ds(pl.multiple_of(start, size), size)

    def narrow(full_rows, seat):
        kept = full_rows[:, :LANES]
        pair = seat // 2
        for q in range(1, pairs):
            kept = jnp.where(pair == q, full_rows[:, q * LANES:(q + 1) * LANES], kept)
        turned = pltpu.roll(kept, rank_size, 1)
        return jnp.where((seat % 2) == upper, kept, turned)

    def pack_rows(twice):
        pieces = []
        for start in range(0, TILE, rows):
            pieces.append(
                jnp.where(upper == 0, twice[start:start + half], twice[start + half:start + rows])
            )
        return jnp.concatenate(pieces, axis=0)

    def unpack_rows(packed):
        packed = packed.astype(f32)
        turned = pltpu.roll(packed, rank_size, 1)
        first = jnp.where(upper == 0, packed, turned)
        second = jnp.where(upper == 0, turned, packed)
        pieces = []
        for start in range(0, TILE // 2, half):
            pieces += [first[start:start + half], second[start:start + half]]
        return jnp.concatenate(pieces, axis=0)

    def project(e, columns, panel):
        def one(tile, carry):
            seat = chosen(column_positions(tile), seats)
            full_rows = dot(columns[at(tile * TILE, TILE), :], panel[...], 1, 1)
            part[e, at(tile * (TILE // 2), TILE // 2), :] = pack_rows(
                narrow(full_rows, seat)
            ).astype(bf16)
            return carry

        lax.fori_loop(0, length // TILE, one, 0)

    def start_sum(e):
        def one(k, carry):
            p = lax.rem(me + k, n)
            pltpu.make_async_remote_copy(
                src_ref=part.at[e, at(p * half, half)], dst_ref=gathered.at[e, me],
                send_sem=rs_send.at[e], recv_sem=rs_recv.at[e],
                device_id={"seq": p}, device_id_type=MESH,
            ).start()
            return carry

        lax.fori_loop(1, n, one, 0)

    def share_sum(e):
        all_bytes(gathered.at[e, pl.ds(0, n - 1)], rs_recv.at[e])

        def add(k, running):
            return running + gathered[e, lax.rem(me + k, n)].astype(f32)

        summed = lax.fori_loop(1, n, add, part[e, at(me * half, half), :].astype(f32))
        low[e, at(me * half, half), :] = summed.astype(bf16)

        def one(k, carry):
            own = low.at[e, at(me * half, half)]
            pltpu.make_async_remote_copy(
                src_ref=own, dst_ref=own, send_sem=ag_send.at[e], recv_sem=ag_recv.at[e],
                device_id={"seq": lax.rem(me + k, n)}, device_id_type=MESH,
            ).start()
            return carry

        lax.fori_loop(1, n, one, 0)

    def low_bytes(e):
        return low.at[e, pl.ds(0, (n - 1) * half)]

    def wait_sum(e):
        all_bytes(low_bytes(e), ag_recv.at[e])

    def low_tile(e, tile):
        return unpack_rows(low[e, at(tile * (TILE // 2), TILE // 2), :])

    def widen_across(e):
        def one(tile, carry):
            low_turned = low_tile(e, tile).T
            positions = tile * TILE + lax.broadcasted_iota(jnp.int32, (1, TILE), 1)
            seat = chosen(positions, seats)
            for q in range(pairs):
                wide[pl.ds(q * LANES, LANES), at(tile * TILE, TILE)] = jnp.where(
                    seat == 2 * q + upper_row, low_turned, 0.0
                ).astype(bf16)
            return carry

        lax.fori_loop(0, length // TILE, one, 0)

    returns = ((dqd, rqd_ref), (dqu, rqu_ref), (dod, rod_ref), (dou, rou_ref))

    def outer(i, columns):
        target, landing = returns[i]
        step = min(TILE, target.shape[1])

        def one(c, carry):
            target[:, at(c * step, step)] = (
                adapter_scale * dot(wide[...], columns[:, at(c * step, step)])
            ).astype(bf16)
            return carry

        lax.fori_loop(0, target.shape[1] // step, one, 0)

        def send(k, carry):
            p = lax.rem(mine + k, groups)
            pltpu.make_async_remote_copy(
                src_ref=target.at[at(p * block, block)], dst_ref=landing.at[mine],
                send_sem=ret_send.at[i], recv_sem=ret_recv.at[i],
                device_id={"head": p}, device_id_type=MESH,
            ).start()
            return carry

        lax.fori_loop(1, groups, send, 0)
        pltpu.make_async_copy(
            target.at[at(mine * block, block)], landing.at[mine], ret_local.at[i]
        ).start()

    wait_panels(3)
    wait_tokens(0)
    project(0, gc, pou)
    start_sum(0)
    send_tokens(5)
    share_sum(0)
    wait_panels(2)
    wait_panels(1)
    wait_sum(0)
    for i in range(1, 5):
        wait_tokens(i)
    send_tokens(6)

    def attend(tile, carry):
        here = at(tile * TILE, TILE)
        positions = column_positions(tile)
        seat = chosen(positions, seats)
        start = chosen(positions, offsets)
        low_rows = low_tile(0, tile)
        widened = jnp.concatenate(
            [jnp.where(seat == 2 * q + upper, low_rows, 0.0).astype(bf16) for q in range(pairs)],
            axis=1,
        )
        heads_grad = (
            fc[here, :].astype(f32) + adapter_scale * dot(widened, pod[...])
        ).astype(bf16)
        keys = kc[pl.ds(pl.multiple_of(tile * TILE, TILE), window), :]
        values = vc[pl.ds(pl.multiple_of(tile * TILE, TILE), window), :]
        key_pos = tile * TILE - span + lax.broadcasted_iota(jnp.int32, (1, window), 1)
        allowed = (key_pos >= start) & (key_pos <= positions)
        for h in range(heads_here):
            lanes = slice(h * HD, (h + 1) * HD)
            scores = dot(qc[here, lanes], keys, 1, 1) * factor
            scores = jnp.where(allowed, scores, big_negative)
            weights = jnp.exp(scores - jnp.max(scores, axis=1, keepdims=True))
            weights = weights * (1.0 / jnp.sum(weights, axis=1, keepdims=True))
            prob_grad = dot(heads_grad[:, lanes], values, 1, 1)
            inner = jnp.sum(weights * prob_grad, axis=1, keepdims=True)
            score_grad = (weights * (prob_grad - inner)).astype(bf16)
            qg[here, lanes] = (dot(score_grad, keys) * factor).astype(bf16)
        full_rows = dot(qg[here, :], pqu[...], 1, 1)
        part[1, at(tile * (TILE // 2), TILE // 2), :] = pack_rows(
            narrow(full_rows, seat)
        ).astype(bf16)
        return carry

    lax.fori_loop(0, length // TILE, attend, 0)
    start_sum(1)

    wait_tokens(5)
    project(2, ac, pod)
    start_sum(2)
    widen_across(0)
    outer(2, ac)
    share_sum(1)
    share_sum(2)
    wait_sum(2)
    widen_across(2)
    outer(3, gc)
    wait_panels(0)
    wait_sum(1)
    wait_tokens(6)
    project(3, xc, pqd)
    start_sum(3)
    widen_across(1)
    outer(0, xc)
    share_sum(3)
    wait_sum(3)
    widen_across(3)
    outer(1, qg)

    for i in range(7):
        all_bytes(token_bytes(i), tok_send.at[i])
    for i in range(4):
        all_bytes(panels[i][2].at[pl.ds(0, (groups - 1) * block)], pan_send.at[i])
        all_bytes(gathered.at[i, pl.ds(0, n - 1)], rs_send.at[i])
        all_bytes(low_bytes(i), ag_send.at[i])
    for i in (2, 3, 0, 1):
        landing = returns[i][1]
        all_bytes(landing.at[pl.ds(0, groups - 1)], ret_recv.at[i])
        all_bytes(landing.at[0], ret_local.at[i])
        all_bytes(landing.at[pl.ds(0, groups - 1)], ret_send.at[i])


def settle_kernel(slots_dev, rank_size, use_ref, map_ref, *refs):
    groups, used = use_ref.shape
    slot = lax.axis_index("head") * slots_dev + pl.program_id(0)
    owner = lax.axis_index("head")
    found, places = [], []
    for m in range(groups):
        count, place, hit_any = jnp.int32(0), jnp.int32(0), jnp.int32(0)
        for i in range(used):
            other = map_ref[use_ref[m, i]]
            hit = other == slot
            place = jnp.where(hit, count, place)
            hit_any = jnp.where(hit, 1, hit_any)
            count = count + jnp.where(other // slots_dev == owner, 1, 0)
        found.append(hit_any.astype(f32))
        places.append(place)
    for source, target in zip(refs[:4], refs[4:]):
        total = jnp.zeros((rank_size, target.shape[2]), f32)
        for m in range(groups):
            rows = pl.ds(pl.multiple_of(places[m] * rank_size, rank_size), rank_size)
            total = total + source[m, rows, :].astype(f32) * found[m]
        target[0] = total


def shards(mesh, *arguments):
    layer_input, _, attention_out = arguments[:3]
    n, groups = mesh.shape["seq"], mesh.shape["head"]
    stores = arguments[10:]
    slots_dev, rank_size = stores[0].shape[:2]
    use_list, store_map = arguments[8], arguments[9]
    rows = layer_input.shape[1]
    length = n * rows
    wide_columns, narrow_columns = layer_input.shape[2] // n, attention_out.shape[2] // n
    block = CAP * rank_size
    span = length // 4
    widths = [store.shape[2] for store in stores]
    vmem = pltpu.VMEM
    dma = pltpu.SemaphoreType.DMA
    anywhere = pl.BlockSpec(memory_space=pl.ANY)
    scalars = pl.BlockSpec(memory_space=pltpu.SMEM)
    scratch = [
        vmem((length, wide_columns), bf16),
        vmem((length, wide_columns), bf16),
        vmem((length, narrow_columns), bf16),
        vmem((length, narrow_columns), bf16),
        vmem((length, narrow_columns), bf16),
        vmem((span + length, HD), bf16),
        vmem((span + length, HD), bf16),
    ]
    scratch += [vmem(store.shape, f32) for store in stores]
    for _ in range(3):
        scratch += [vmem((groups * block, width), bf16) for width in widths]
    scratch += [
        vmem((4, length // 2, LANES), bf16),
        vmem((4, n, rows // 2, LANES), bf16),
        vmem((4, length // 2, LANES), bf16),
        vmem((groups * block, length), bf16),
        vmem((length, narrow_columns), bf16),
        dma((4,)), dma((7,)), dma((7,)), dma((7,)),
        dma((4,)), dma((4,)), dma((4,)),
        dma((4,)), dma((4,)), dma((4,)), dma((4,)),
        dma((4,)), dma((4,)), dma((4,)),
    ]
    returned = pl.pallas_call(
        functools.partial(gradient_kernel, n, groups),
        out_shape=[jax.ShapeDtypeStruct((groups, block, width), bf16) for width in widths],
        in_specs=[anywhere] * 7 + [scalars] * 3 + [anywhere] * 4,
        out_specs=[anywhere] * 4,
        scratch_shapes=scratch,
        compiler_params=pltpu.CompilerParams(
            collective_id=0, has_side_effects=True, vmem_limit_bytes=60 * 1024 * 1024
        ),
        cost_estimate=pl.CostEstimate(
            flops=12_000_000_000, bytes_accessed=24_000_000, transcendentals=2_000_000
        ),
        name="adapter_backward",
    )(*arguments)
    return tuple(
        pl.pallas_call(
            functools.partial(settle_kernel, slots_dev, rank_size),
            grid=(slots_dev,),
            out_shape=[jax.ShapeDtypeStruct(store.shape, f32) for store in stores],
            in_specs=[scalars] * 2 + [pl.BlockSpec(memory_space=pltpu.VMEM)] * 4,
            out_specs=[
                pl.BlockSpec((1, rank_size, width), lambda s: (s, 0, 0)) for width in widths
            ],
            compiler_params=pltpu.CompilerParams(vmem_limit_bytes=32 * 1024 * 1024),
            name="settle_slots",
        )(use_list, store_map, *returned)
    )


def solution(mesh):
    token_rows = P("head", "seq", None)
    store = P("head", None, "seq")
    return jax.shard_map(
        functools.partial(shards, mesh),
        mesh=mesh,
        in_specs=(token_rows,) * 7 + (P("head", None), P(), P()) + (store,) * 4,
        out_specs=(store,) * 4,
        check_vma=False,
    )
```

time: 588 us -> 239 us (0.41); the launches traced: 578 us -> 239 us
  waiting for transfers between devices: 315 us -> 0 us
  Pallas kernels: 0 us -> 234 us
  matrix products: 79.1 us -> 0 us
  starting transfers between devices: 68.6 us -> 0 us
  local copies, waits for them, and re-layouts: 67.7 us -> 4.53 us
  other arithmetic: 25.2 us -> 0 us
  between operations: 14.7 us -> 0.69 us
  loops' own time: 8.21 us -> 0 us
    pallas_call x0 -> x2, Pallas kernels: none -> 234 us  [the longest x1 228 us: shards(): pl.pallas_call(functools.partial(gradient_kernel, n, groups), out_shape=[...]
    all_to_all x13 -> x0, waiting for transfers between devices: 179 us -> none  [the longest x1 50.5 us: shards(): lax.all_to_all(out_grad[0], 'seq', split_axis=1, concat_axis=0, tiled=True)]
    psum x2 -> x0, waiting for transfers between devices: 135 us -> none  [the longest x1 71.7 us: shards(): low_rank_back = lax.psum(partial_back.astype(jnp.bfloat16), 'seq')]
    dot_general x31 -> x0, matrix products: 79.1 us -> none  [the longest x8 14.5 us: contract_axes(): lax.dot_general(left_side, right_side, (((left_dim,), (right_dim,)), ((),...]
    all_to_all x13 -> x0, starting transfers between devices: 68 us -> none  [the longest x1 6.68 us: shards(): lax.all_to_all(frozen_output_grad[0], 'seq', split_axis=1, concat_axis=0,...]
    unnamed x71 -> x12, local copies, waits for them, and re-layouts: 28.1 us -> 4.53 us
    convert_element_type x11 -> x0, local copies, waits for them, and re-layouts: 15.7 us -> none  [the longest x4 5.64 us: pack_slots(): jnp.einsum('mcl,lrw->mcrw', select, store_part, precision=highest)]
    sub x3 -> x0, other arithmetic: 15.4 us -> none  [the longest x2 15.4 us: one_block(): weights = jnp.exp(scores - row_max)]
  transfers between devices with their start and end apart: 17 -> 0, of which waited for: 14 -> 0; matrix products, arithmetic and copies ran while one was open for 17% -> 0% of each run, Pallas kernels for 0% -> 0%
where the time goes in v1:
time: 239 us
  Pallas kernels  234 us (98%)
  local copies, waits for them, and re-layouts  4.53 us (2%)
    pallas_call x1, Pallas kernels, shards(): pl.pallas_call(functools.partial(gradient_kernel, n, groups), out_shape=[...  228 us
    pallas_call x1, Pallas kernels, shards(): pl.pallas_call(functools.partial(settle_kernel, slots_dev, rank_size), gr...  6.12 us

profile of v1, /device:TPU:1, one launch (start us, length us, event | category | flops | bytes accessed | tf_op | source)
XLA Modules:
  0.0 239.0 jit_solution(13832913550100451513)
XLA Ops:
  0.6 0.0 copy-start.5
  0.6 0.0 copy-start.4
  0.7 227.7 %adapter_backward.1 = (bf16[4,128,1024]{2,1,0:T(8,128)(2,1)}, bf16[4,128,512]{2,1,0:T(8,128)(2,1)}, bf16[4,128,512]{2,1,0:T(8,128)(2,1)}, bf16[4,128,1024]{2,1,0:T(8,128)(2,1)}) custom-call(bf16[1,128,8192]{2,1,0:T(8,128)(2,1)} %x_ref.1, bf16[1,128,8192]{2,1,0:T(8,128)(2,1)} %g_ref.1, bf16[1,128,4096]{2,1,0:T(8,128)(2,1)} %a_ref.1, ...), custom_call_target="tpu_custom_call" | custom-call | flops 12000000000 | bytes 24000000 | tf_op jit(solution)/shard_map/adapter_backward/pallas_call | solution.py:477
  228.3 0.0 copy-done.5
  228.3 0.0 copy-done.4
  228.3 0.0 copy-start
  228.4 1.2 copy-done
  229.6 0.0 copy-start.1
  229.6 1.2 copy-done.1
  230.8 0.0 copy-start.2
  230.8 1.0 copy-done.2
  231.8 0.0 copy-start.3
  231.8 1.0 copy-done.3
  232.9 6.1 %settle_slots.1 = (f32[8,64,1024]{2,1,0:T(8,128)}, f32[8,64,512]{2,1,0:T(8,128)}, f32[8,64,512]{2,1,0:T(8,128)}, f32[8,64,1024]{2,1,0:T(8,128)}) custom-call(s32[4,8]{1,0:T(4,128)S(1)} %copy-done.4, s32[32]{0:T(128)S(1)} %copy-done.5, bf16[4,128,1024]{2,1,0:T(8,128)(2,1)S(1)} %copy-done, bf16[4,128,512]{2,1,0:T(8,128)(2,1)S(1)} %copy-done.2, ...), custom_call_target="tpu_custom_call" | custom-call | tf_op jit(solution)/shard_map/settle_slots/pallas_call | solution.py:492
Async XLA Ops:
  0.6 227.7 %copy-start.5 = (s32[32]{0:T(128)S(1)}, s32[32]{0:T(128)}, u32[]{:S(2)}) copy-start(s32[32]{0:T(128)} %map_ref.3) | copy-start | bytes 388
  0.6 227.7 %copy-start.4 = (s32[4,8]{1,0:T(4,128)S(1)}, s32[4,8]{1,0:T(4,128)}, u32[]{:S(2)}) copy-start(s32[4,8]{1,0:T(4,128)} %use_ref.3) | copy-start | bytes 388
  228.3 1.2 copy-start
  229.6 1.2 copy-start.1
  230.8 1.0 copy-start.2
  231.8 1.0 copy-start.3

commit v2 on v1

--- a/solution.py
+++ b/solution.py
@@ -99,15 +99,18 @@
         (x_ref, xc, 0, None),
     )
 
-    def send_tokens(i):
+    def send_tokens(i, piece=0, pieces=1):
         source, target, first, head_of = tokens[i]
         width = target.shape[1]
+        count = rows // pieces
 
         def view(p):
             column = p if head_of is None else head_of(p)
-            return source.at[0, :, pl.ds(pl.multiple_of(column * width, LANES), width)]
-
-        landing = target.at[pl.ds(pl.multiple_of(first + me * rows, rows), rows)]
+            return source.at[
+                0, pl.ds(piece * count, count), pl.ds(pl.multiple_of(column * width, LANES), width)
+            ]
+
+        landing = target.at[pl.ds(pl.multiple_of(first + me * rows + piece * count, count), count)]
 
         def one(k, carry):
             p = lax.rem(me + k, n)
@@ -130,8 +133,8 @@
         all_bytes(token_bytes(i), tok_recv.at[i])
         all_bytes(tokens[i][1].at[pl.ds(0, rows)], tok_local.at[i])
 
-    for i in range(5):
-        send_tokens(i)
+    send_tokens(0)
+    send_tokens(1)
     kc[pl.ds(0, span), :] = jnp.zeros((span, HD), bf16)
     vc[pl.ds(0, span), :] = jnp.zeros((span, HD), bf16)
 
@@ -287,13 +290,13 @@
     def low_tile(e, tile):
         return unpack_rows(low[e, at(tile * (TILE // 2), TILE // 2), :])
 
-    def widen_across(e):
+    def widen_across(e, slot=0):
         def one(tile, carry):
             low_turned = low_tile(e, tile).T
             positions = tile * TILE + lax.broadcasted_iota(jnp.int32, (1, TILE), 1)
             seat = chosen(positions, seats)
             for q in range(pairs):
-                wide[pl.ds(q * LANES, LANES), at(tile * TILE, TILE)] = jnp.where(
+                wide[slot, pl.ds(q * LANES, LANES), at(tile * TILE, TILE)] = jnp.where(
                     seat == 2 * q + upper_row, low_turned, 0.0
                 ).astype(bf16)
             return carry
@@ -302,13 +305,13 @@
 
     returns = ((dqd, rqd_ref), (dqu, rqu_ref), (dod, rod_ref), (dou, rou_ref))
 
-    def outer(i, columns):
+    def outer(i, columns, slot=0):
         target, landing = returns[i]
         step = min(TILE, target.shape[1])
 
         def one(c, carry):
             target[:, at(c * step, step)] = (
-                adapter_scale * dot(wide[...], columns[:, at(c * step, step)])
+                adapter_scale * dot(wide[slot], columns[:, at(c * step, step)])
             ).astype(bf16)
             return carry
 
@@ -332,14 +335,17 @@
     wait_tokens(0)
     project(0, gc, pou)
     start_sum(0)
+    for i in (2, 3, 4):
+        send_tokens(i)
+    share_sum(0)
     send_tokens(5)
-    share_sum(0)
     wait_panels(2)
     wait_panels(1)
-    wait_sum(0)
     for i in range(1, 5):
         wait_tokens(i)
-    send_tokens(6)
+    wait_sum(0)
+    send_tokens(6, 0, 4)
+    send_tokens(6, 1, 4)
 
     def attend(tile, carry):
         here = at(tile * TILE, TILE)
@@ -376,24 +382,25 @@
 
     lax.fori_loop(0, length // TILE, attend, 0)
     start_sum(1)
-
     wait_tokens(5)
     project(2, ac, pod)
     start_sum(2)
+    send_tokens(6, 2, 4)
     widen_across(0)
     outer(2, ac)
     share_sum(1)
     share_sum(2)
+    send_tokens(6, 3, 4)
     wait_sum(2)
     widen_across(2)
     outer(3, gc)
+    wait_sum(1)
+    widen_across(1, 1)
     wait_panels(0)
-    wait_sum(1)
     wait_tokens(6)
     project(3, xc, pqd)
     start_sum(3)
-    widen_across(1)
-    outer(0, xc)
+    outer(0, xc, 1)
     share_sum(3)
     wait_sum(3)
     widen_across(3)
@@ -414,25 +421,26 @@
 
 def settle_kernel(slots_dev, rank_size, use_ref, map_ref, *refs):
     groups, used = use_ref.shape
-    slot = lax.axis_index("head") * slots_dev + pl.program_id(0)
     owner = lax.axis_index("head")
-    found, places = [], []
-    for m in range(groups):
-        count, place, hit_any = jnp.int32(0), jnp.int32(0), jnp.int32(0)
+    for target in refs[4:]:
+        target[...] = jnp.zeros(target.shape, f32)
+
+    def add_batch(m, carry):
+        count = jnp.int32(0)
         for i in range(used):
-            other = map_ref[use_ref[m, i]]
-            hit = other == slot
-            place = jnp.where(hit, count, place)
-            hit_any = jnp.where(hit, 1, hit_any)
-            count = count + jnp.where(other // slots_dev == owner, 1, 0)
-        found.append(hit_any.astype(f32))
-        places.append(place)
-    for source, target in zip(refs[:4], refs[4:]):
-        total = jnp.zeros((rank_size, target.shape[2]), f32)
-        for m in range(groups):
-            rows = pl.ds(pl.multiple_of(places[m] * rank_size, rank_size), rank_size)
-            total = total + source[m, rows, :].astype(f32) * found[m]
-        target[0] = total
+            slot = map_ref[use_ref[m, i]]
+            hit = slot // slots_dev == owner
+
+            @pl.when(hit)
+            def _(slot=slot, count=count):
+                rows = pl.ds(pl.multiple_of(count * rank_size, rank_size), rank_size)
+                for source, target in zip(refs[:4], refs[4:]):
+                    target[slot % slots_dev] += source[m, rows, :].astype(f32)
+
+            count = count + jnp.where(hit, 1, 0)
+        return carry
+
+    lax.fori_loop(0, groups, add_batch, 0)
 
 
 def shards(mesh, *arguments):
@@ -447,6 +455,7 @@
     block = CAP * rank_size
     span = length // 4
     widths = [store.shape[2] for store in stores]
+    pieces = max(1, min(widths) // LANES)
     vmem = pltpu.VMEM
     dma = pltpu.SemaphoreType.DMA
     anywhere = pl.BlockSpec(memory_space=pl.ANY)
@@ -467,7 +476,7 @@
         vmem((4, length // 2, LANES), bf16),
         vmem((4, n, rows // 2, LANES), bf16),
         vmem((4, length // 2, LANES), bf16),
-        vmem((groups * block, length), bf16),
+        vmem((2, groups * block, length), bf16),
         vmem((length, narrow_columns), bf16),
         dma((4,)), dma((7,)), dma((7,)), dma((7,)),
         dma((4,)), dma((4,)), dma((4,)),
@@ -491,11 +500,13 @@
     return tuple(
         pl.pallas_call(
             functools.partial(settle_kernel, slots_dev, rank_size),
-            grid=(slots_dev,),
+            grid=(pieces,),
             out_shape=[jax.ShapeDtypeStruct(store.shape, f32) for store in stores],
-            in_specs=[scalars] * 2 + [pl.BlockSpec(memory_space=pltpu.VMEM)] * 4,
+            in_specs=[scalars] * 2
+            + [pl.BlockSpec((groups, block, width // pieces), lambda s: (0, 0, s)) for width in widths],
             out_specs=[
-                pl.BlockSpec((1, rank_size, width), lambda s: (s, 0, 0)) for width in widths
+                pl.BlockSpec((slots_dev, rank_size, width // pieces), lambda s: (0, 0, s))
+                for width in widths
             ],
             compiler_params=pltpu.CompilerParams(vmem_limit_bytes=32 * 1024 * 1024),
             name="settle_slots",

time: 239 us -> 233 us (0.975)
  Pallas kernels: 234 us -> 227 us
    pallas_call x1, Pallas kernels: 228 us -> 222 us  [shards(): pl.pallas_call(functools.partial(gradient_kernel, n, groups), out_shape=[...]
where the time goes in v2:
time: 233 us
  Pallas kernels  227 us (97%)
  local copies, waits for them, and re-layouts  4.53 us (2%)
    pallas_call x1, Pallas kernels, shards(): pl.pallas_call(functools.partial(gradient_kernel, n, groups), out_shape=[...  222 us
    pallas_call x1, Pallas kernels, shards(): pl.pallas_call(functools.partial(settle_kernel, slots_dev, rank_size), gr...  5.72 us

profile of v2, /device:TPU:1, one launch (start us, length us, event | category | flops | bytes accessed | tf_op | source)
XLA Modules:
  0.0 232.7 jit_solution(13252246125197507636)
XLA Ops:
  0.6 0.0 copy-start.5
  0.6 0.0 copy-start.4
  0.7 221.8 %adapter_backward.1 = (bf16[4,128,1024]{2,1,0:T(8,128)(2,1)}, bf16[4,128,512]{2,1,0:T(8,128)(2,1)}, bf16[4,128,512]{2,1,0:T(8,128)(2,1)}, bf16[4,128,1024]{2,1,0:T(8,128)(2,1)}) custom-call(bf16[1,128,8192]{2,1,0:T(8,128)(2,1)} %x_ref.1, bf16[1,128,8192]{2,1,0:T(8,128)(2,1)} %g_ref.1, bf16[1,128,4096]{2,1,0:T(8,128)(2,1)} %a_ref.1, ...), custom_call_target="tpu_custom_call" | custom-call | flops 12000000000 | bytes 24000000 | tf_op jit(solution)/shard_map/adapter_backward/pallas_call | solution.py:486
  222.4 0.0 copy-done.5
  222.4 0.0 copy-done.4
  222.4 0.0 copy-start
  222.5 1.2 copy-done
  223.7 0.0 copy-start.1
  223.7 1.2 copy-done.1
  224.9 0.0 copy-start.2
  224.9 1.0 copy-done.2
  225.9 0.0 copy-start.3
  225.9 1.0 copy-done.3
  227.0 5.7 %settle_slots.1 = (f32[8,64,1024]{2,1,0:T(8,128)}, f32[8,64,512]{2,1,0:T(8,128)}, f32[8,64,512]{2,1,0:T(8,128)}, f32[8,64,1024]{2,1,0:T(8,128)}) custom-call(s32[4,8]{1,0:T(4,128)S(1)} %copy-done.4, s32[32]{0:T(128)S(1)} %copy-done.5, bf16[4,128,1024]{2,1,0:T(8,128)(2,1)S(1)} %copy-done, bf16[4,128,512]{2,1,0:T(8,128)(2,1)S(1)} %copy-done.2, ...), custom_call_target="tpu_custom_call" | custom-call | tf_op jit(solution)/shard_map/settle_slots/pallas_call | solution.py:501
Async XLA Ops:
  0.6 221.8 %copy-start.5 = (s32[32]{0:T(128)S(1)}, s32[32]{0:T(128)}, u32[]{:S(2)}) copy-start(s32[32]{0:T(128)} %map_ref.3) | copy-start | bytes 388
  0.6 221.8 %copy-start.4 = (s32[4,8]{1,0:T(4,128)S(1)}, s32[4,8]{1,0:T(4,128)}, u32[]{:S(2)}) copy-start(s32[4,8]{1,0:T(4,128)} %use_ref.3) | copy-start | bytes 388
  222.4 1.2 copy-start
  223.7 1.2 copy-start.1
  224.9 1.0 copy-start.2
  225.9 1.0 copy-start.3
